TPU v7x, 256 devices: a whole 4x4x8 slice. The times are simulated.
256 devices in a mesh: group: 8 (over z), shard: 32 (over x, y, core).
Axes of the slice: x: 4, y: 4, z: 8, core: 2. Of those that a mesh axis runs over, the one named last changes fastest.
Arguments:
- gradient: float32 [37748736], P(('group', 'shard')), may hold values from -3000 to 3000
- momentum: float32 [37748736], P(('group', 'shard')), may hold values from -6 to 6
- master_weights: float32 [37748736], P(('group', 'shard')), may hold values from -0.3125 to 0.3125
- slot_table: int32 [24], replicated, may hold values from 0 to 23, as said below
Outputs:
- new_momentum: float32 [37748736], P(('group', 'shard'))
- update: float32 [37748736], P(('group', 'shard'))
- new_master: float32 [37748736], P(('group', 'shard'))
- weights: bfloat16 [37748736], P('group')
Inputs may be any that keep to these rules, and one draw needn't show every extreme that they name: `slot_table`: each of 0 to 23 appears exactly once.
All inputs are finite; a program needn't handle non-finite values.
Results may differ from a plain program's by a relative error of at most 0.0066.
Values may be sent and summed in bfloat16 or wider, within the bound.
No kernel may reach another device: no remote copies, remote signals or barrier semaphores. Data moves between devices by JAX's collectives and lax.ppermute only.
A program may use at most 64 MiB of HBM per device.

v0:
```python
import math

import jax
import jax.numpy as jnp
from jax import lax
from jax.sharding import PartitionSpec as P

D = 2048
FF = 768
NS_ITERS = 2


coef_first = 3.4445
coef_second = -4.775
coef_third = 2.0315
beta_momentum = 0.95
learn_rate = 0.02
weight_decay = 0.1


def shifted(block, axis, distance):
    devices = range(lax.axis_size(axis))
    route = [(i - distance, i) for i in devices if i - distance in devices]
    return lax.ppermute(block, axis, route)


def newton_schulz(flat, kind):
    tall = flat.reshape(D, FF).T
    wide = flat.reshape(FF, D)
    matrix = jnp.where(kind == 2, wide, tall)
    values = matrix.astype(jnp.float32)
    magnitude = jnp.sqrt(jnp.sum(values * values))
    state = (values / (magnitude + 1e-07)).astype(jnp.bfloat16)
    for counter in range(NS_ITERS):
        gram = jnp.dot(state, state.T, preferred_element_type=jnp.float32).astype(jnp.bfloat16)
        square = jnp.dot(gram, gram, preferred_element_type=jnp.float32)
        poly = (coef_second * gram.astype(jnp.float32) + coef_third * square).astype(jnp.bfloat16)
        state = (
            coef_first * state.astype(jnp.float32)
            + jnp.dot(poly, state, preferred_element_type=jnp.float32)
        ).astype(jnp.bfloat16)
    return jnp.where(kind == 2, state.reshape(-1), state.T.reshape(-1))


def on_device(gradient, momentum, master_weights, slot_table):
    shard_len = gradient.shape[0]
    matrix_len = D * FF
    shards = lax.axis_size("shard")
    group_id = lax.axis_index("group")
    shard_id = lax.axis_index("shard")
    total_count = shard_len * shards * lax.axis_size("group")
    total_sq = lax.psum(jnp.sum(gradient * gradient), ("group", "shard"))
    clip_factor = jnp.minimum(1.0, 0.5 * math.sqrt(total_count) / jnp.sqrt(total_sq + 1e-06))
    clipped = clip_factor * gradient
    new_momentum = beta_momentum * momentum + clipped
    looked = (clipped + beta_momentum * new_momentum).astype(jnp.bfloat16)
    own_slot = jnp.int32(0)
    is_owner = jnp.bool_(False)
    for local_slot in range(3):
        first_shard = local_slot * matrix_len // shard_len
        matched = shard_id == first_shard
        own_slot = jnp.where(matched, jnp.int32(local_slot), own_slot)
        is_owner = is_owner | matched
    global_slot = 3 * group_id + own_slot
    indices = jnp.arange(slot_table.shape[0], dtype=jnp.int32)
    kind = jnp.sum(jnp.where(slot_table == global_slot, indices % 3, 0))
    base = own_slot * matrix_len
    span = -(-matrix_len // shard_len) + 1
    direct_rel = jnp.clip(base - shard_id * shard_len, 0, span * shard_len - matrix_len)
    arrivals = [looked]
    for hop in range(1, span):
        arrivals.append(shifted(looked, "shard", -hop))
    gathered = lax.dynamic_slice_in_dim(jnp.concatenate(arrivals), direct_rel, matrix_len)
    solved = lax.cond(
        is_owner,
        lambda matrix: newton_schulz(matrix, kind),
        lambda matrix: jnp.zeros_like(matrix),
        gathered,
    )
    laid_out = lax.dynamic_update_slice_in_dim(
        jnp.zeros((span * shard_len,), jnp.bfloat16), solved, direct_rel, 0
    )
    total_piece = laid_out[:shard_len].astype(jnp.float32)
    for hop in range(1, span):
        returned = shifted(laid_out[hop * shard_len : (hop + 1) * shard_len], "shard", hop)
        total_piece = total_piece + returned.astype(jnp.float32)
    update = math.sqrt(D) * total_piece
    new_master = master_weights * (1.0 - learn_rate * weight_decay) - learn_rate * 0.2 * update
    weights = lax.all_gather(new_master.astype(jnp.bfloat16), "shard", axis=0, tiled=True)
    return (new_momentum, update, new_master, weights)


def solution(mesh):
    in_specs = (P(("group", "shard")), P(("group", "shard")), P(("group", "shard")), P())
    out_specs = (P(("group", "shard")), P(("group", "shard")), P(("group", "shard")), P("group"))
    return jax.shard_map(
        on_device, mesh=mesh, in_specs=in_specs, out_specs=out_specs, check_vma=False
    )
```

profile of v0, /device:TPU:1, one launch (start us, length us, event | category | flops | bytes accessed | tf_op | source)
XLA Modules:
  0.0 450.7 jit_solution(3458352336477998404)
XLA Ops:
  7.2 1.8 multiply_reduce_fusion
  9.0 81.4 %psum.7 = f32[]{:T(128)} all-reduce(f32[]{:T(128)} %multiply_reduce_fusion), channel_id=1, replica_groups=mesh['group'=8,'shard'=32] {'group','shard'}, use_global_device_ids=true, to_apply=%region_1.0 | all-reduce | flops 1 | bytes 8 | tf_op jit(solution)/shard_map/psum | solution.py:52
  91.1 2.3 constant_dynamic-update-slice_fusion.11
  93.4 2.8 collective-permute-start
  96.2 1.3 collective-permute-start.10
  97.5 1.3 collective-permute-start.9
  101.4 14.9 %collective-permute-done = bf16[147456]{0:T(1024)(128)(2,1)} collective-permute-done((bf16[147456]{0:T(1024)(128)(2,1)}, bf16[147456]{0:T(1024)(128)(2,1)}, u32[]{:S(2)}, u32[]{:S(2)}) %collective-permute-start) | collective-permute-done | bytes 294944 | tf_op jit(solution)/shard_map/ppermute | solution.py:24
  118.6 7.1 %collective-permute-done.1 = bf16[147456]{0:T(1024)(128)(2,1)S(1)} collective-permute-done((bf16[147456]{0:T(1024)(128)(2,1)}, bf16[147456]{0:T(1024)(128)(2,1)S(1)}, u32[]{:S(2)}, u32[]{:S(2)}) %collective-permute-start.1) | collective-permute-done | bytes 294944 | tf_op jit(solution)/shard_map/ppermute | solution.py:24
  127.0 8.4 %collective-permute-done.2 = bf16[147456]{0:T(1024)(128)(2,1)S(1)} collective-permute-done((bf16[147456]{0:T(1024)(128)(2,1)}, bf16[147456]{0:T(1024)(128)(2,1)S(1)}, u32[]{:S(2)}, u32[]{:S(2)}) %collective-permute-start.2) | collective-permute-done | bytes 294944 | tf_op jit(solution)/shard_map/ppermute | solution.py:24
  136.7 12.3 %collective-permute-done.3 = bf16[147456]{0:T(1024)(128)(2,1)S(1)} collective-permute-done((bf16[147456]{0:T(1024)(128)(2,1)}, bf16[147456]{0:T(1024)(128)(2,1)S(1)}, u32[]{:S(2)}, u32[]{:S(2)}) %collective-permute-start.3) | collective-permute-done | bytes 294944 | tf_op jit(solution)/shard_map/ppermute | solution.py:24
  150.3 10.8 %collective-permute-done.4 = bf16[147456]{0:T(1024)(128)(2,1)S(1)} collective-permute-done((bf16[147456]{0:T(1024)(128)(2,1)}, bf16[147456]{0:T(1024)(128)(2,1)S(1)}, u32[]{:S(2)}, u32[]{:S(2)}) %collective-permute-start.4) | collective-permute-done | bytes 294944 | tf_op jit(solution)/shard_map/ppermute | solution.py:24
  162.5 8.7 %collective-permute-done.5 = bf16[147456]{0:T(1024)(128)(2,1)S(1)} collective-permute-done((bf16[147456]{0:T(1024)(128)(2,1)}, bf16[147456]{0:T(1024)(128)(2,1)S(1)}, u32[]{:S(2)}, u32[]{:S(2)}) %collective-permute-start.5) | collective-permute-done | bytes 294944 | tf_op jit(solution)/shard_map/ppermute | solution.py:24
  172.5 13.3 %collective-permute-done.6 = bf16[147456]{0:T(1024)(128)(2,1)S(1)} collective-permute-done((bf16[147456]{0:T(1024)(128)(2,1)}, bf16[147456]{0:T(1024)(128)(2,1)S(1)}, u32[]{:S(2)}, u32[]{:S(2)}) %collective-permute-start.6) | collective-permute-done | bytes 294944 | tf_op jit(solution)/shard_map/ppermute | solution.py:24
  190.3 1.7 copy-done
  192.2 48.5 %dynamic_update_slice.3 = bf16[1769472]{0:T(1024)(128)(2,1)S(1)} dynamic-update-slice(bf16[1769472]{0:T(1024)(128)(2,1)S(1)} %broadcast_in_dim.5, bf16[1572864]{0:T(1024)(128)(2,1)} %copy-done, s32[]{:T(128)} %min.4) | dynamic-update-slice | bytes 6291460 | tf_op jit(solution)/shard_map/dynamic_update_slice | solution.py:80
  241.0 1.9 collective-permute-start.11
  242.9 11.1 %collective-permute-start.21 = (bf16[147456]{0:T(1024)(128)(2,1)S(1)}, bf16[147456]{0:T(1024)(128)(2,1)S(1)}, u32[]{:S(2)}, u32[]{:S(2)}) collective-permute-start(bf16[147456]{0:T(1024)(128)(2,1)S(1)} %get-tuple-element.145), channel_id=1, source_target_pairs={{0,11},{1,12},{2,13},{3,14},{4,15},{5,16},{6,17},{7,18},{8,19},{9,... | collective-permute-start | bytes 884744 | tf_op jit(solution)/shard_map/ppermute | solution.py:24
  254.0 3.1 collective-permute-start.20
  257.2 66.7 %collective-permute-start.19 = (bf16[147456]{0:T(1024)(128)(2,1)S(1)}, bf16[147456]{0:T(1024)(128)(2,1)S(1)}, u32[]{:S(2)}, u32[]{:S(2)}) collective-permute-start(bf16[147456]{0:T(1024)(128)(2,1)S(1)} %get-tuple-element.147), channel_id=1, source_target_pairs={{0,9},{1,10},{2,11},{3,12},{4,13},{5,14},{6,15},{7,16},{8,17},{9,1... | collective-permute-start | bytes 884744 | tf_op jit(solution)/shard_map/ppermute | solution.py:24
  323.8 1.6 collective-permute-start.18
  325.5 1.3 collective-permute-start.17
  326.8 1.3 collective-permute-start.16
  328.2 4.6 %collective-permute-start.15 = (bf16[147456]{0:T(1024)(128)(2,1)S(1)}, bf16[147456]{0:T(1024)(128)(2,1)S(1)}, u32[]{:S(2)}, u32[]{:S(2)}) collective-permute-start(bf16[147456]{0:T(1024)(128)(2,1)S(1)} %get-tuple-element.151), channel_id=1, source_target_pairs={{0,5},{1,6},{2,7},{3,8},{4,9},{5,10},{6,11},{7,12},{8,13},{9,14},{... | collective-permute-start | bytes 884744 | tf_op jit(solution)/shard_map/ppermute | solution.py:24
  332.8 8.6 %collective-permute-start.14 = (bf16[147456]{0:T(1024)(128)(2,1)S(1)}, bf16[147456]{0:T(1024)(128)(2,1)S(1)}, u32[]{:S(2)}, u32[]{:S(2)}) collective-permute-start(bf16[147456]{0:T(1024)(128)(2,1)S(1)} %get-tuple-element.152), channel_id=1, source_target_pairs={{0,4},{1,5},{2,6},{3,7},{4,8},{5,9},{6,10},{7,11},{8,12},{9,13},{1... | collective-permute-start | bytes 884744 | tf_op jit(solution)/shard_map/ppermute | solution.py:24
  341.4 1.3 collective-permute-start.13
  342.7 8.4 %collective-permute-start.12 = (bf16[147456]{0:T(1024)(128)(2,1)S(1)}, bf16[147456]{0:T(1024)(128)(2,1)S(1)}, u32[]{:S(2)}, u32[]{:S(2)}) collective-permute-start(bf16[147456]{0:T(1024)(128)(2,1)S(1)} %get-tuple-element.154), channel_id=1, source_target_pairs={{0,2},{1,3},{2,4},{3,5},{4,6},{5,7},{6,8},{7,9},{8,10},{9,11},{10,... | collective-permute-start | bytes 884744 | tf_op jit(solution)/shard_map/ppermute | solution.py:24
  351.1 3.1 collective-permute-done.13
  354.2 3.5 collective-permute-done.12
  357.6 1.6 fusion.7
  359.3 1.9 broadcast_multiply_fusion
  361.2 73.6 %all-gather.2.cloned.1.call-done = bf16[4718592]{0:T(1024)(128)(2,1)} async-done(((bf16[147456]{0:T(1024)(128)(2,1)}), bf16[4718592]{0:T(1024)(128)(2,1)}) %all-gather.2.cloned.1.call-update) | async-done | bytes 9437200 | tf_op jit(solution)/shard_map/all_gather | solution.py:89
  434.8 9.1 %copy.29 = bf16[4718592]{0:T(1024)(128)(2,1)} copy(bf16[4718592]{0:T(1024)(128)(2,1)} %all-gather.2.cloned.1.call-done) | data formatting | bytes 18874368
  (44 shorter events, 16.6 us)
Async XLA Ops:
  7.2 427.6 %all-gather.2.cloned.1.call-start = ((), (), s32[]{:S(2)}) async-start(), calls=%async_computation | async-start | bytes 9732096 | tf_op jit(solution)/shard_map/all_gather | solution.py:89
  93.4 22.9 %collective-permute-start = (bf16[147456]{0:T(1024)(128)(2,1)}, bf16[147456]{0:T(1024)(128)(2,1)}, u32[]{:S(2)}, u32[]{:S(2)}) collective-permute-start(bf16[147456]{0:T(1024)(128)(2,1)} %get-tuple-element.142), channel_id=1, source_target_pairs={{1,0},{2,1},{3,2},{4,3},{5,4},{6,5},{7,6},{8,7},{9,8},{10,9},{11,1... | collective-permute-start | bytes 884744 | tf_op jit(solution)/shard_map/ppermute | solution.py:24
  96.2 92.6 %collective-permute-start.10 = (bf16[147456]{0:T(1024)(128)(2,1)}, bf16[147456]{0:T(1024)(128)(2,1)}, u32[]{:S(2)}, u32[]{:S(2)}) collective-permute-start(bf16[147456]{0:T(1024)(128)(2,1)} %get-tuple-element.142), channel_id=1, source_target_pairs={{11,0},{12,1},{13,2},{14,3},{15,4},{16,5},{17,6},{18,7},{19,8},{20... | collective-permute-start | bytes 884744 | tf_op jit(solution)/shard_map/ppermute | solution.py:24
  97.5 90.3 %collective-permute-start.9 = (bf16[147456]{0:T(1024)(128)(2,1)}, bf16[147456]{0:T(1024)(128)(2,1)}, u32[]{:S(2)}, u32[]{:S(2)}) collective-permute-start(bf16[147456]{0:T(1024)(128)(2,1)} %get-tuple-element.142), channel_id=1, source_target_pairs={{10,0},{11,1},{12,2},{13,3},{14,4},{15,5},{16,6},{17,7},{18,8},{19... | collective-permute-start | bytes 884744 | tf_op jit(solution)/shard_map/ppermute | solution.py:24
  98.8 88.0 %collective-permute-start.8 = (bf16[147456]{0:T(1024)(128)(2,1)}, bf16[147456]{0:T(1024)(128)(2,1)}, u32[]{:S(2)}, u32[]{:S(2)}) collective-permute-start(bf16[147456]{0:T(1024)(128)(2,1)} %get-tuple-element.142), channel_id=1, source_target_pairs={{9,0},{10,1},{11,2},{12,3},{13,4},{14,5},{15,6},{16,7},{17,8},{18,... | collective-permute-start | bytes 884744 | tf_op jit(solution)/shard_map/ppermute | solution.py:24
  100.1 85.7 %collective-permute-start.7 = (bf16[147456]{0:T(1024)(128)(2,1)}, bf16[147456]{0:T(1024)(128)(2,1)}, u32[]{:S(2)}, u32[]{:S(2)}) collective-permute-start(bf16[147456]{0:T(1024)(128)(2,1)} %get-tuple-element.142), channel_id=1, source_target_pairs={{8,0},{9,1},{10,2},{11,3},{12,4},{13,5},{14,6},{15,7},{16,8},{17,9... | collective-permute-start | bytes 884744 | tf_op jit(solution)/shard_map/ppermute | solution.py:24
  116.3 9.4 %collective-permute-start.1 = (bf16[147456]{0:T(1024)(128)(2,1)}, bf16[147456]{0:T(1024)(128)(2,1)S(1)}, u32[]{:S(2)}, u32[]{:S(2)}) collective-permute-start(bf16[147456]{0:T(1024)(128)(2,1)} %get-tuple-element.142), channel_id=1, source_target_pairs={{2,0},{3,1},{4,2},{5,3},{6,4},{7,5},{8,6},{9,7},{10,8},{11,9},{12,... | collective-permute-start | bytes 884744 | tf_op jit(solution)/shard_map/ppermute | solution.py:24
  117.6 72.2 %copy-start.3 = (s32[24]{0:T(128)S(1)}, s32[24]{0:T(128)}, u32[]{:S(2)}) copy-start(s32[24]{0:T(128)} %param.9) | copy-start | bytes 292
  125.6 9.7 %collective-permute-start.2 = (bf16[147456]{0:T(1024)(128)(2,1)}, bf16[147456]{0:T(1024)(128)(2,1)S(1)}, u32[]{:S(2)}, u32[]{:S(2)}) collective-permute-start(bf16[147456]{0:T(1024)(128)(2,1)} %get-tuple-element.142), channel_id=1, source_target_pairs={{3,0},{4,1},{5,2},{6,3},{7,4},{8,5},{9,6},{10,7},{11,8},{12,9},{13... | collective-permute-start | bytes 884744 | tf_op jit(solution)/shard_map/ppermute | solution.py:24
  135.4 13.6 %collective-permute-start.3 = (bf16[147456]{0:T(1024)(128)(2,1)}, bf16[147456]{0:T(1024)(128)(2,1)S(1)}, u32[]{:S(2)}, u32[]{:S(2)}) collective-permute-start(bf16[147456]{0:T(1024)(128)(2,1)} %get-tuple-element.142), channel_id=1, source_target_pairs={{4,0},{5,1},{6,2},{7,3},{8,4},{9,5},{10,6},{11,7},{12,8},{13,9},{1... | collective-permute-start | bytes 884744 | tf_op jit(solution)/shard_map/ppermute | solution.py:24
  149.0 12.2 %collective-permute-start.4 = (bf16[147456]{0:T(1024)(128)(2,1)}, bf16[147456]{0:T(1024)(128)(2,1)S(1)}, u32[]{:S(2)}, u32[]{:S(2)}) collective-permute-start(bf16[147456]{0:T(1024)(128)(2,1)} %get-tuple-element.142), channel_id=1, source_target_pairs={{5,0},{6,1},{7,2},{8,3},{9,4},{10,5},{11,6},{12,7},{13,8},{14,9},{... | collective-permute-start | bytes 884744 | tf_op jit(solution)/shard_map/ppermute | solution.py:24
  161.1 10.0 %collective-permute-start.5 = (bf16[147456]{0:T(1024)(128)(2,1)}, bf16[147456]{0:T(1024)(128)(2,1)S(1)}, u32[]{:S(2)}, u32[]{:S(2)}) collective-permute-start(bf16[147456]{0:T(1024)(128)(2,1)} %get-tuple-element.142), channel_id=1, source_target_pairs={{6,0},{7,1},{8,2},{9,3},{10,4},{11,5},{12,6},{13,7},{14,8},{15,9},... | collective-permute-start | bytes 884744 | tf_op jit(solution)/shard_map/ppermute | solution.py:24
  171.2 14.6 %collective-permute-start.6 = (bf16[147456]{0:T(1024)(128)(2,1)}, bf16[147456]{0:T(1024)(128)(2,1)S(1)}, u32[]{:S(2)}, u32[]{:S(2)}) collective-permute-start(bf16[147456]{0:T(1024)(128)(2,1)} %get-tuple-element.142), channel_id=1, source_target_pairs={{7,0},{8,1},{9,2},{10,3},{11,4},{12,5},{13,6},{14,7},{15,8},{16,9}... | collective-permute-start | bytes 884744 | tf_op jit(solution)/shard_map/ppermute | solution.py:24
  190.3 1.7 copy-start
  240.7 116.9 %copy-start.2 = (f32[147456]{0:T(1024)S(1)}, f32[147456]{0:T(1024)}, u32[]{:S(2)}) copy-start(f32[147456]{0:T(1024)} %param.8) | copy-start | bytes 1769476
  241.0 84.5 %collective-permute-start.11 = (bf16[147456]{0:T(1024)(128)(2,1)S(1)}, bf16[147456]{0:T(1024)(128)(2,1)S(1)}, u32[]{:S(2)}, u32[]{:S(2)}) collective-permute-start(bf16[147456]{0:T(1024)(128)(2,1)S(1)} %get-tuple-element.144), channel_id=1, source_target_pairs={{0,1},{1,2},{2,3},{3,4},{4,5},{5,6},{6,7},{7,8},{8,9},{9,10},{10,1... | collective-permute-start | bytes 884744 | tf_op jit(solution)/shard_map/ppermute | solution.py:24
  242.9 83.9 %collective-permute-start.21 = (bf16[147456]{0:T(1024)(128)(2,1)S(1)}, bf16[147456]{0:T(1024)(128)(2,1)S(1)}, u32[]{:S(2)}, u32[]{:S(2)}) collective-permute-start(bf16[147456]{0:T(1024)(128)(2,1)S(1)} %get-tuple-element.145), channel_id=1, source_target_pairs={{0,11},{1,12},{2,13},{3,14},{4,15},{5,16},{6,17},{7,18},{8,19},{9,... | collective-permute-start | bytes 884744 | tf_op jit(solution)/shard_map/ppermute | solution.py:24
  254.0 74.1 %collective-permute-start.20 = (bf16[147456]{0:T(1024)(128)(2,1)S(1)}, bf16[147456]{0:T(1024)(128)(2,1)S(1)}, u32[]{:S(2)}, u32[]{:S(2)}) collective-permute-start(bf16[147456]{0:T(1024)(128)(2,1)S(1)} %get-tuple-element.146), channel_id=1, source_target_pairs={{0,10},{1,11},{2,12},{3,13},{4,14},{5,15},{6,16},{7,17},{8,18},{9,... | collective-permute-start | bytes 884744 | tf_op jit(solution)/shard_map/ppermute | solution.py:24
  257.2 75.6 %collective-permute-start.19 = (bf16[147456]{0:T(1024)(128)(2,1)S(1)}, bf16[147456]{0:T(1024)(128)(2,1)S(1)}, u32[]{:S(2)}, u32[]{:S(2)}) collective-permute-start(bf16[147456]{0:T(1024)(128)(2,1)S(1)} %get-tuple-element.147), channel_id=1, source_target_pairs={{0,9},{1,10},{2,11},{3,12},{4,13},{5,14},{6,15},{7,16},{8,17},{9,1... | collective-permute-start | bytes 884744 | tf_op jit(solution)/shard_map/ppermute | solution.py:24
  323.8 17.5 %collective-permute-start.18 = (bf16[147456]{0:T(1024)(128)(2,1)S(1)}, bf16[147456]{0:T(1024)(128)(2,1)S(1)}, u32[]{:S(2)}, u32[]{:S(2)}) collective-permute-start(bf16[147456]{0:T(1024)(128)(2,1)S(1)} %get-tuple-element.148), channel_id=1, source_target_pairs={{0,8},{1,9},{2,10},{3,11},{4,12},{5,13},{6,14},{7,15},{8,16},{9,17... | collective-permute-start | bytes 884744 | tf_op jit(solution)/shard_map/ppermute | solution.py:24
  325.5 17.2 %collective-permute-start.17 = (bf16[147456]{0:T(1024)(128)(2,1)S(1)}, bf16[147456]{0:T(1024)(128)(2,1)S(1)}, u32[]{:S(2)}, u32[]{:S(2)}) collective-permute-start(bf16[147456]{0:T(1024)(128)(2,1)S(1)} %get-tuple-element.149), channel_id=1, source_target_pairs={{0,7},{1,8},{2,9},{3,10},{4,11},{5,12},{6,13},{7,14},{8,15},{9,16}... | collective-permute-start | bytes 884744 | tf_op jit(solution)/shard_map/ppermute | solution.py:24
  326.8 24.2 %collective-permute-start.16 = (bf16[147456]{0:T(1024)(128)(2,1)S(1)}, bf16[147456]{0:T(1024)(128)(2,1)S(1)}, u32[]{:S(2)}, u32[]{:S(2)}) collective-permute-start(bf16[147456]{0:T(1024)(128)(2,1)S(1)} %get-tuple-element.150), channel_id=1, source_target_pairs={{0,6},{1,7},{2,8},{3,9},{4,10},{5,11},{6,12},{7,13},{8,14},{9,15},... | collective-permute-start | bytes 884744 | tf_op jit(solution)/shard_map/ppermute | solution.py:24
  328.2 22.9 %collective-permute-start.15 = (bf16[147456]{0:T(1024)(128)(2,1)S(1)}, bf16[147456]{0:T(1024)(128)(2,1)S(1)}, u32[]{:S(2)}, u32[]{:S(2)}) collective-permute-start(bf16[147456]{0:T(1024)(128)(2,1)S(1)} %get-tuple-element.151), channel_id=1, source_target_pairs={{0,5},{1,6},{2,7},{3,8},{4,9},{5,10},{6,11},{7,12},{8,13},{9,14},{... | collective-permute-start | bytes 884744 | tf_op jit(solution)/shard_map/ppermute | solution.py:24
  332.8 18.3 %collective-permute-start.14 = (bf16[147456]{0:T(1024)(128)(2,1)S(1)}, bf16[147456]{0:T(1024)(128)(2,1)S(1)}, u32[]{:S(2)}, u32[]{:S(2)}) collective-permute-start(bf16[147456]{0:T(1024)(128)(2,1)S(1)} %get-tuple-element.152), channel_id=1, source_target_pairs={{0,4},{1,5},{2,6},{3,7},{4,8},{5,9},{6,10},{7,11},{8,12},{9,13},{1... | collective-permute-start | bytes 884744 | tf_op jit(solution)/shard_map/ppermute | solution.py:24
  341.4 12.8 %collective-permute-start.13 = (bf16[147456]{0:T(1024)(128)(2,1)S(1)}, bf16[147456]{0:T(1024)(128)(2,1)S(1)}, u32[]{:S(2)}, u32[]{:S(2)}) collective-permute-start(bf16[147456]{0:T(1024)(128)(2,1)S(1)} %get-tuple-element.153), channel_id=1, source_target_pairs={{0,3},{1,4},{2,5},{3,6},{4,7},{5,8},{6,9},{7,10},{8,11},{9,12},{10... | collective-permute-start | bytes 884744 | tf_op jit(solution)/shard_map/ppermute | solution.py:24
  342.7 14.9 %collective-permute-start.12 = (bf16[147456]{0:T(1024)(128)(2,1)S(1)}, bf16[147456]{0:T(1024)(128)(2,1)S(1)}, u32[]{:S(2)}, u32[]{:S(2)}) collective-permute-start(bf16[147456]{0:T(1024)(128)(2,1)S(1)} %get-tuple-element.154), channel_id=1, source_target_pairs={{0,2},{1,3},{2,4},{3,5},{4,6},{5,7},{6,8},{7,9},{8,10},{9,11},{10,... | collective-permute-start | bytes 884744 | tf_op jit(solution)/shard_map/ppermute | solution.py:24
Sparse Core Ops, SparseCore 0:
  359.4 75.3 all-gather.1
where the time goes:
time: 456 us; the launch traced here: 451 us
  waiting for transfers between devices  156 us (34%)
  starting transfers between devices  126 us (28%)
  blocking collectives  81.4 us (18%)
  local copies, waits for them, and re-layouts  65.1 us (14%)
  between operations  15.2 us (3%)
  other arithmetic  7.64 us (2%)
    ppermute x22, starting transfers between devices, shifted(): return lax.ppermute(block, axis, route)  126 us
    ppermute x22, waiting for transfers between devices, shifted(): return lax.ppermute(block, axis, route)  82 us
    psum x1, blocking collectives, on_device(): total_sq = lax.psum(jnp.sum(gradient * gradient), ('group', 'shard'))  81.4 us
    all_gather x1, waiting for transfers between devices, on_device(): lax.all_gather(new_master.astype(jnp.bfloat16), 'shard', axis=0, tiled=True)  73.6 us
    dynamic_update_slice x1, local copies, waits for them, and re-layouts, on_device(): lax.dynamic_update_slice_in_dim(jnp.zeros((span * shard_len,), jnp.bfloat...  48.5 us
    unnamed x17, local copies, waits for them, and re-layouts  14.8 us
  transfers between devices with their start and end apart: 23, of which 10 were waited for; matrix products, arithmetic and copies ran while one was open for 1% of the time, Pallas kernels for 0%

commit v1 on v0

v1 whole, which is shorter than its diff:
```python
import math

import jax
import jax.numpy as jnp
from jax import lax
from jax.experimental import pallas as pl
from jax.experimental.pallas import tpu as pltpu
from jax.sharding import PartitionSpec as P

D = 2048
FF = 768
MATS = 3
UNITS = 32
SHARD_TILES = 72
SHARD_ROWS = 1152
MAT_ROWS = 12288
MAT_TILES = 768
WIDE = 256

coef_first = 3.4445
coef_second = -4.775
coef_third = 2.0315
beta_momentum = 0.95
learn_rate = 0.02
weight_decay = 0.1

f32 = jnp.float32
bf16 = jnp.bfloat16
MIB = 2**20

VM = pl.BlockSpec(memory_space=pltpu.VMEM)
SM = pl.BlockSpec(memory_space=pltpu.SMEM)
ANY = pl.BlockSpec(memory_space=pl.ANY)


def shard_of(x, y, c):
    return (x % 4) * 8 + (y % 4) * 2 + c


def first_route(step):
    route = []
    for x in range(4):
        for y in range(4):
            route.append((shard_of(x, y, 0), shard_of(x, y + step, 0)))
            route.append((shard_of(x, y, 1), shard_of(x + step, y, 1)))
    return route


def second_route(step):
    route = []
    for x in range(4):
        for y in range(4):
            route.append((shard_of(x, y, 0), shard_of(x + step, y, 0)))
            route.append((shard_of(x, y, 1), shard_of(x, y + step, 1)))
    return route


def swap_route():
    return [(s, s ^ 1) for s in range(32)]


def kind_of(info, matrix):
    kind = jnp.int32(0)
    for m in range(24):
        kind = jnp.where(info[m] == matrix, jnp.int32(m % 3), kind)
    return kind


def look_kernel(info, sums, g_ref, m_ref, nm_ref, look_ref, scratch):
    total = jnp.sum(sums[...], axis=0, keepdims=True)[:, :1]
    clip = jnp.minimum(1.0, 0.5 * math.sqrt(24 * D * FF) / jnp.sqrt(total + 1e-06))
    clipped = clip * g_ref[...]
    new_momentum = beta_momentum * m_ref[...] + clipped
    nm_ref[...] = new_momentum
    scratch[...] = clipped + beta_momentum * new_momentum
    group, shard = info[24], info[25]
    for t in range(3):
        kind = kind_of(info, 3 * group + (3 * shard + t) // UNITS)
        row = 384 * t

        @pl.when(kind != 2)
        def _():
            for a in range(4):
                for j in range(6):
                    tile = scratch[pl.ds(row + 96 * a + j, 16, stride=6), :]
                    look_ref[24 * t + 6 * a + j] = tile.astype(bf16)

        @pl.when(kind == 2)
        def _():
            for j in range(16):
                tile = scratch[pl.ds(row + j, 16, stride=16), :]
                look_ref[24 * t + j] = tile.astype(bf16)
            for q in range(8):
                low = scratch[pl.ds(row + 256 + q, 8, stride=16), :]
                high = scratch[pl.ds(row + 264 + q, 8, stride=16), :]
                look_ref[24 * t + 16 + q] = jnp.concatenate([low, high], 0).astype(bf16)


def tiles(x, first, count, stride):
    return jnp.concatenate([x[first + stride * i] for i in range(count)], 0)


def mm(a, b):
    return jnp.dot(a, b, preferred_element_type=f32)


def mm_t(a, b):
    return lax.dot_general(a, b, (((1,), (1,)), ((), ())), preferred_element_type=f32)


def orthogonalize(kind, base, x, wide, flat, a0, b0, wb, b1, total):
    @pl.when(kind == 2)
    def _():
        def pair(i, carry):
            t = base + 48 * i
            for h in range(2):
                rows = pl.ds(pl.multiple_of(32 * i + 16 * h, 16), 16)
                for j in range(16):
                    wide[rows, 128 * j : 128 * j + 128] = x[t + 24 * h + j]
            rows = pl.ds(pl.multiple_of(512 + 16 * i, 16), 16)
            for q in range(8):
                one = x[t + 16 + q].astype(f32)
                two = x[t + 40 + q].astype(f32)
                low = jnp.concatenate([one[:8], two[:8]], 0).astype(bf16)
                high = jnp.concatenate([one[8:], two[8:]], 0).astype(bf16)
                wide[rows, 128 * q : 128 * q + 128] = low
                wide[rows, 128 * (q + 8) : 128 * (q + 8) + 128] = high
            return carry

        lax.fori_loop(0, 16, pair, 0)

    @pl.when(kind != 2)
    def _():
        def chunk(i, carry):
            columns = pl.ds(pl.multiple_of(WIDE * i, WIDE), WIDE)
            for j in range(6):
                wide[128 * j : 128 * j + 128, columns] = tiles(x, base + 96 * i + j, 16, 6).T
            return carry

        lax.fori_loop(0, 8, chunk, 0)

    parts = [slice(WIDE * n, WIDE * n + WIDE) for n in range(3)]
    iota = lax.broadcasted_iota
    square_sum = jnp.zeros((1, 1), f32)
    for part in parts:
        total[:, part] = mm_t(wide[...], wide[part, :])
        block = total[part, part]
        same = iota(jnp.int32, (WIDE, WIDE), 0) == iota(jnp.int32, (WIDE, WIDE), 1)
        square_sum = square_sum + jnp.sum(jnp.where(same, block, 0.0), keepdims=True)
    inverse = 1.0 / (jnp.sqrt(square_sum) + 1e-07)
    for part in parts:
        a0[part, :] = (total[part, :] * inverse * inverse).astype(bf16)
    for part in parts:
        square = mm(a0[...], a0[:, part])
        b0[:, part] = (coef_second * a0[:, part].astype(f32) + coef_third * square).astype(bf16)
    for part in parts:
        step = coef_first * a0[:, part].astype(f32) + mm(a0[...], b0[:, part])
        total[:, part] = coef_first * step
        wb[:, part] = step.astype(bf16)
    a1 = a0
    for part in parts:
        a1[:, part] = (total[:, part] + mm(b0[...], wb[:, part])).astype(bf16)
    for part in parts:
        square = mm(a1[...], a1[:, part])
        b1[:, part] = (coef_second * a1[:, part].astype(f32) + coef_third * square).astype(bf16)
    scale = inverse * math.sqrt(D)
    rest = wb
    diagonal_row = []
    diagonal_column = jnp.zeros((FF, 1), f32)
    for n, part in enumerate(parts):
        both = b0[:, part].astype(f32) + b1[:, part].astype(f32)
        step = coef_first * both + mm(b1[...], b0[:, part])
        same = iota(jnp.int32, (FF, WIDE), 0) == iota(jnp.int32, (FF, WIDE), 1) + WIDE * n
        diagonal = jnp.where(same, step, 0.0)
        diagonal_row.append(jnp.sum(diagonal, axis=0, keepdims=True))
        diagonal_column = diagonal_column + jnp.sum(diagonal, axis=1, keepdims=True)
        rest[:, part] = jnp.where(same, 0.0, step).astype(bf16)
    diagonal_row = (jnp.concatenate(diagonal_row, 1) + coef_first * coef_first) * scale
    diagonal_column = (diagonal_column + coef_first * coef_first) * scale

    @pl.when(kind != 2)
    def _():
        def chunk(i, carry):
            block = jnp.concatenate([tiles(x, base + 96 * i + j, 16, 6) for j in range(6)], 1)
            moved = mm(block, rest[...]) * scale + block.astype(f32) * diagonal_row
            for j in range(6):
                rows = pl.ds(SHARD_ROWS + 1536 * i + j, WIDE, stride=6)
                flat[rows, :] = moved[:, 128 * j : 128 * j + 128]
            return carry

        lax.fori_loop(0, 8, chunk, 0)

    @pl.when(kind == 2)
    def _():
        def chunk(i, carry):
            block = wide[:, pl.ds(pl.multiple_of(WIDE * i, WIDE), WIDE)]
            moved = mm(rest[...], block) * scale + block.astype(f32) * diagonal_column
            for h in range(2):
                panel = moved[:, 128 * h : 128 * h + 128]
                start = SHARD_ROWS + 2 * i + h
                for u in range(UNITS):
                    rows = pl.ds(start + 384 * u, 16, stride=16)
                    flat[rows, :] = panel[16 * u : 16 * u + 16]
                    rows = pl.ds(start + 384 * u + 256, 8, stride=16)
                    flat[rows, :] = panel[512 + 8 * u : 512 + 8 * u + 8]
            return carry

        lax.fori_loop(0, 8, chunk, 0)


def matrix_kernel(last, n_sources, *refs):
    info, sources, refs = refs[0], refs[1 : 1 + n_sources], refs[1 + n_sources :]
    if last:
        master, _, weights, own = refs[:4]
        refs = refs[4:]
    else:
        master, weights, sent, own, other = refs[:5]
        refs = refs[5:]
    x, wide, flat, a0, b0, wb, b1, total, master_block, out_block, sems, more = refs
    group, shard = info[24], info[25]
    row, column, core = shard // 8, (shard // 2) % 4, shard % 2
    matrix = jnp.int32(2) if last else core
    first = (UNITS * matrix) // 3
    final = (UNITS * matrix + UNITS - 1) // 3
    matrix_rows = pl.ds(pl.multiple_of(MAT_ROWS * matrix, MAT_ROWS), MAT_ROWS)
    load_master = pltpu.make_async_copy(master.at[matrix_rows, :], master_block, more.at[0])
    load_master.start()

    loads = []
    for i, source in enumerate(sources):
        partner, (second, first_hops) = divmod(i, 8)[0], PLACES[i % 8]
        holder = core if partner == 0 else 1 - core
        for slot, hops in enumerate(first_hops):
            at_zero = shard_of(row - second + 4, column - hops + 4, 0)
            at_one = shard_of(row - hops + 4, column - second + 4, 1)
            place = jnp.where(holder == 0, at_zero, at_one)
            wanted = (place >= first) & (place <= final)
            target = SHARD_TILES * jnp.clip(place - first, 0, 11)
            copy = pltpu.make_async_copy(
                source.at[pl.ds(SHARD_TILES * slot, SHARD_TILES)],
                x.at[pl.ds(target, SHARD_TILES)],
                sems.at[2 * i + slot],
            )
            loads.append((wanted, copy))
    for wanted, copy in loads:
        pl.when(wanted)(copy.start)
    for wanted, copy in loads:
        pl.when(wanted)(copy.wait)

    kind = kind_of(info, 3 * group + matrix)
    base = MAT_TILES * matrix - SHARD_TILES * first
    orthogonalize(kind, base, x, wide, flat, a0, b0, wb, b1, total)

    def piece(who, out, sem):
        start = jnp.clip(SHARD_ROWS * (who + 1) - MAT_ROWS * matrix, 0, MAT_ROWS + SHARD_ROWS)
        start = pl.multiple_of(start, 128)
        return pltpu.make_async_copy(flat.at[pl.ds(start, SHARD_ROWS), :], out, sem)

    stores = [piece(shard, own, more.at[1])]
    if not last:
        stores.append(piece(shard + 1 - 2 * core, other, more.at[2]))
    for store in stores:
        store.start()
    load_master.wait()

    def weigh(i, carry):
        rows = pl.ds(pl.multiple_of(512 * i, 512), 512)
        update = flat[pl.ds(pl.multiple_of(SHARD_ROWS + 512 * i, 128), 512), :]
        kept = master_block[rows, :].astype(f32) * (1.0 - learn_rate * weight_decay)
        out_block[rows, :] = (kept - learn_rate * 0.2 * update).astype(bf16)
        return carry

    lax.fori_loop(0, MAT_ROWS // 512, weigh, 0)
    store = pltpu.make_async_copy(out_block, weights.at[matrix_rows, :], more.at[3])
    store.start()
    stores.append(store)
    if not last:
        store = pltpu.make_async_copy(out_block, sent, more.at[4])
        store.start()
        stores.append(store)
    for store in stores:
        store.wait()


PLACES = [
    (0, (0, 1)),
    (0, (2, 3)),
    (1, (0, 1)),
    (1, (2, 3)),
    (3, (0, 1)),
    (3, (2, 3)),
    (2, (0, 1)),
    (2, (2, 3)),
]

MATRIX_SCRATCH = [
    pltpu.VMEM((12 * SHARD_TILES, 16, 128), bf16),
    pltpu.VMEM((FF, D), bf16),
    pltpu.VMEM((MAT_ROWS + 2 * SHARD_ROWS, 128), f32),
    pltpu.VMEM((FF, FF), bf16),
    pltpu.VMEM((FF, FF), bf16),
    pltpu.VMEM((FF, FF), bf16),
    pltpu.VMEM((FF, FF), bf16),
    pltpu.VMEM((FF, FF), f32),
    pltpu.VMEM((MAT_ROWS, 128), bf16),
    pltpu.VMEM((MAT_ROWS, 128), bf16),
    pltpu.SemaphoreType.DMA((32,)),
    pltpu.SemaphoreType.DMA((5,)),
]


def finish_kernel(info, _, received, mine, theirs, third, master_ref, weights, update_ref, new_ref, sems):
    shard = info[25]
    core = shard % 2
    start = MAT_ROWS * (1 - core)
    quarter = MAT_ROWS // 4
    copies = []
    for i in range(4):
        rows = pl.ds(pl.multiple_of(start + quarter * i, quarter), quarter)
        copy = pltpu.make_async_copy(
            received.at[pl.ds(quarter * i, quarter), :], weights.at[rows, :], sems.at[i]
        )
        copy.start()
        copies.append(copy)
    for t in range(3):
        matrix = (3 * shard + t) // UNITS
        rows = slice(384 * t, 384 * t + 384)

        @pl.when(matrix == core)
        def _():
            update_ref[rows, :] = mine[rows, :]

        @pl.when(matrix == 1 - core)
        def _():
            update_ref[rows, :] = theirs[rows, :]

        @pl.when(matrix == 2)
        def _():
            update_ref[rows, :] = third[rows, :]

    kept = master_ref[...] * (1.0 - learn_rate * weight_decay)
    new_ref[...] = kept - learn_rate * 0.2 * update_ref[...]
    for copy in copies:
        copy.wait()


def params(mib):
    return pltpu.CompilerParams(vmem_limit_bytes=mib * MIB)


def on_device(gradient, momentum, master_weights, slot_table):
    place = jnp.stack([lax.axis_index("group"), lax.axis_index("shard")]).astype(jnp.int32)
    info = jnp.concatenate([slot_table, place])
    gathered = lax.all_gather(master_weights.astype(bf16), "shard", axis=0, tiled=True)
    gathered = gathered.reshape(MATS * MAT_ROWS, 128)

    own_sq = jnp.sum(gradient * gradient)
    sums = lax.all_to_all(jnp.full((32, 128), own_sq, f32), "shard", 0, 0)
    sums = jnp.broadcast_to(jnp.sum(sums, axis=0, keepdims=True), (8, 128))
    sums = lax.all_to_all(sums, "group", 0, 0)

    flat_shape = jax.ShapeDtypeStruct((SHARD_ROWS, 128), f32)
    new_momentum, look = pl.pallas_call(
        look_kernel,
        out_shape=(flat_shape, jax.ShapeDtypeStruct((SHARD_TILES, 16, 128), bf16)),
        in_specs=[SM, VM, VM, VM],
        out_specs=(VM, VM),
        scratch_shapes=[pltpu.VMEM((SHARD_ROWS, 128), f32)],
        compiler_params=params(8),
    )(info, sums, gradient.reshape(SHARD_ROWS, 128), momentum.reshape(SHARD_ROWS, 128))

    def send(block, route):
        return lax.ppermute(block, "shard", route)

    near = send(look, first_route(1))
    far = send(look, first_route(2))
    back = send(look, first_route(3))
    ahead = jnp.concatenate([look, near])
    behind = jnp.concatenate([far, back])
    sources = [ahead, behind]
    forward = [send(ahead, second_route(1)), send(behind, second_route(1))]
    backward = [send(ahead, second_route(3)), send(behind, second_route(3))]
    across = [send(forward[0], second_route(1)), send(backward[1], second_route(3))]
    sources = sources + forward + backward + across
    sources = sources + [send(block, swap_route()) for block in sources]

    weights_shape = jax.ShapeDtypeStruct((MATS * MAT_ROWS, 128), bf16)
    cost = pl.CostEstimate(flops=9_300_000_000, bytes_accessed=20_000_000, transcendentals=0)
    weights, sent, mine, other = pl.pallas_call(
        lambda *refs: matrix_kernel(False, 16, *refs),
        out_shape=(weights_shape, jax.ShapeDtypeStruct((MAT_ROWS, 128), bf16), flat_shape, flat_shape),
        in_specs=[SM] + [ANY] * 17,
        out_specs=(ANY, ANY, ANY, ANY),
        scratch_shapes=MATRIX_SCRATCH,
        compiler_params=params(60),
        cost_estimate=cost,
    )(info, *sources, gathered)
    received = send(sent, swap_route())
    theirs = send(other, swap_route())
    weights, third = pl.pallas_call(
        lambda *refs: matrix_kernel(True, 16, *refs),
        out_shape=(weights_shape, flat_shape),
        in_specs=[SM] + [ANY] * 18,
        out_specs=(ANY, ANY),
        scratch_shapes=MATRIX_SCRATCH,
        input_output_aliases={18: 0},
        compiler_params=params(60),
        cost_estimate=cost,
    )(info, *sources, gathered, weights)
    weights, update, new_master = pl.pallas_call(
        finish_kernel,
        out_shape=(weights_shape, flat_shape, flat_shape),
        in_specs=[SM, ANY, VM, VM, VM, VM, VM],
        out_specs=(ANY, VM, VM),
        scratch_shapes=[pltpu.SemaphoreType.DMA((4,))],
        input_output_aliases={1: 0},
        compiler_params=params(16),
    )(info, weights, received, mine, theirs, third, master_weights.reshape(SHARD_ROWS, 128))
    return (
        new_momentum.reshape(-1),
        update.reshape(-1),
        new_master.reshape(-1),
        weights.reshape(-1),
    )


def solution(mesh):
    in_specs = (P(("group", "shard")), P(("group", "shard")), P(("group", "shard")), P())
    out_specs = (P(("group", "shard")), P(("group", "shard")), P(("group", "shard")), P("group"))
    return jax.shard_map(
        on_device, mesh=mesh, in_specs=in_specs, out_specs=out_specs, check_vma=False
    )
```

time: 456 us -> 160 us (0.35); the launches traced: 451 us -> 160 us
  waiting for transfers between devices: 156 us -> 46.3 us
  starting transfers between devices: 126 us -> 36.9 us
  blocking collectives: 81.4 us -> 0 us
  local copies, waits for them, and re-layouts: 65.1 us -> 8.41 us
  Pallas kernels: 0 us -> 49.4 us
    ppermute x22 -> x19, starting transfers between devices: 126 us -> 20.1 us  [send(): return lax.ppermute(block, 'shard', route)]
    psum x1 -> x0, blocking collectives: 81.4 us -> none  [on_device(): total_sq = lax.psum(jnp.sum(gradient * gradient), ('group', 'shard'))]
    all_gather x1, waiting for transfers between devices: 73.6 us -> 0.01 us  [on_device(): lax.all_gather(master_weights.astype(bf16), 'shard', axis=0, tiled=True)]
    pallas_call x0 -> x4, Pallas kernels: none -> 49.4 us  [the longest x1 22.8 us: on_device(): pl.pallas_call(lambda *refs: matrix_kernel(False, 16, *refs), out_shape=(...]
    dynamic_update_slice x1 -> x0, local copies, waits for them, and re-layouts: 48.5 us -> none  [on_device(): lax.dynamic_update_slice_in_dim(jnp.zeros((span * shard_len,), jnp.bfloat...]
    ppermute x22 -> x19, waiting for transfers between devices: 82 us -> 33.7 us  [send(): return lax.ppermute(block, 'shard', route)]
    all_to_all x0 -> x2, starting transfers between devices: none -> 16.8 us  [the longest x1 8.59 us: on_device(): sums = lax.all_to_all(jnp.full((32, 128), own_sq, f32), 'shard', 0, 0)]
    all_to_all x0 -> x2, waiting for transfers between devices: none -> 12.6 us  [the longest x1 6.86 us: on_device(): sums = lax.all_to_all(jnp.full((32, 128), own_sq, f32), 'shard', 0, 0)]
  transfers between devices with their start and end apart: 23 -> 22, of which waited for: 10 -> 8; matrix products, arithmetic and copies ran while one was open for 1% -> 3% of each run, Pallas kernels for 0% -> 14%
where the time goes in v1:
time: 160 us
  Pallas kernels  49.4 us (31%)
  waiting for transfers between devices  46.3 us (29%)
  starting transfers between devices  36.9 us (23%)
  between operations  14.4 us (9%)
  local copies, waits for them, and re-layouts  8.41 us (5%)
  other arithmetic  4.38 us (3%)
    ppermute x19, waiting for transfers between devices, send(): return lax.ppermute(block, 'shard', route)  33.7 us
    pallas_call x1, Pallas kernels, on_device(): pl.pallas_call(lambda *refs: matrix_kernel(False, 16, *refs), out_shape=(...  22.8 us
    pallas_call x1, Pallas kernels, on_device(): pl.pallas_call(lambda *refs: matrix_kernel(True, 16, *refs), out_shape=(w...  20.9 us
    ppermute x19, starting transfers between devices, send(): return lax.ppermute(block, 'shard', route)  20.1 us
    all_to_all x1, starting transfers between devices, on_device(): sums = lax.all_to_all(jnp.full((32, 128), own_sq, f32), 'shard', 0, 0)  8.59 us
    all_to_all x1, starting transfers between devices, on_device(): sums = lax.all_to_all(sums, 'group', 0, 0)  8.19 us
    all_to_all x1, waiting for transfers between devices, on_device(): sums = lax.all_to_all(jnp.full((32, 128), own_sq, f32), 'shard', 0, 0)  6.86 us
    unnamed x46, local copies, waits for them, and re-layouts  6.48 us
  transfers between devices with their start and end apart: 22, of which 8 were waited for; matrix products, arithmetic and copies ran while one was open for 3% of the time, Pallas kernels for 14%

profile of v1, /device:TPU:1, one launch (start us, length us, event | category | flops | bytes accessed | tf_op | source)
XLA Modules:
  0.0 159.7 jit_solution(15841010326275979169)
XLA Ops:
  7.2 1.8 %convert_element_type.3 = bf16[147456]{0:T(1024)(128)(2,1)} convert(f32[147456]{0:T(1024)} %param.6) | non-fusion elementwise | flops 147456 | bytes 884736 | tf_op jit(solution)/shard_map/convert_element_type | solution.py:354
  9.0 1.8 %multiply_reduce_fusion = f32[]{:T(128)} fusion(f32[147456]{0:T(1024)} %param.4), kind=kLoop, calls=%fused_computation | loop fusion | flops 294911 | bytes 589828 | tf_op jit(solution)/shard_map/reduce_sum | solution.py:357
  10.9 1.3 broadcast_in_dim.4
  12.1 8.6 %all-to-all-start = ((f32[32,1,128]{2,1,0:T(1,128)}), f32[32,1,128]{2,1,0:T(1,128)S(1)}, u32[]{:S(2)}, u32[]{:S(2)}) async-start(f32[32,1,128]{2,1,0:T(1,128)} %broadcast_in_dim.4), calls=%async_computation | async-start | bytes 32768 | tf_op jit(solution)/shard_map/all_to_all | solution.py:358
  20.7 6.9 %all-to-all-done = f32[32,1,128]{2,1,0:T(1,128)S(1)} async-done(((f32[32,1,128]{2,1,0:T(1,128)}), f32[32,1,128]{2,1,0:T(1,128)S(1)}, u32[]{:S(2)}, u32[]{:S(2)}) %all-to-all-start) | async-done | bytes 16416 | tf_op jit(solution)/shard_map/all_to_all | solution.py:358
  27.6 0.6 broadcast_in_dim.10
  28.2 8.2 %all-to-all-start.1 = ((f32[8,1,128]{2,1,0:T(1,128)}), f32[8,1,128]{2,1,0:T(1,128)S(1)}, u32[]{:S(2)}, u32[]{:S(2)}) async-start(f32[8,1,128]{2,1,0:T(1,128)} %broadcast_in_dim.10), calls=%async_computation.1 | async-start | bytes 8192 | tf_op jit(solution)/shard_map/all_to_all | solution.py:360
  36.4 0.7 pad_add_fusion.info.refs_0_
  37.1 5.7 %all-to-all-done.1 = f32[8,1,128]{2,1,0:T(1,128)S(1)} async-done(((f32[8,1,128]{2,1,0:T(1,128)}), f32[8,1,128]{2,1,0:T(1,128)S(1)}, u32[]{:S(2)}, u32[]{:S(2)}) %all-to-all-start.1) | async-done | bytes 4128 | tf_op jit(solution)/shard_map/all_to_all | solution.py:360
  42.8 1.1 copy-done.1
  43.9 1.1 copy-done.4
  45.0 1.9 %shard_map.75 = (f32[1152,128]{1,0:T(8,128)}, bf16[72,16,128]{2,1,0:T(8,128)(2,1)S(1)}) custom-call(s32[26]{0:T(128)S(1)} %pad_add_fusion.info.refs_0_, f32[8,128]{1,0:T(8,128)S(1)} %bitcast.15, f32[1152,128]{1,0:T(8,128)S(1)} %bitcast.13, f32[1152,128]{1,0:T(8,128)S(1)} %bitcast.14), custom_call_target="tpu_custom_call" | custom-call | tf_op jit(solution)/shard_map/pallas_call | solution.py:363
  47.2 1.6 collective-permute-start.1
  48.8 1.1 collective-permute-start.2
  49.9 8.2 %collective-permute-done = bf16[72,16,128]{2,1,0:T(8,128)(2,1)S(1)} collective-permute-done((bf16[72,16,128]{2,1,0:T(8,128)(2,1)S(1)}, bf16[72,16,128]{2,1,0:T(8,128)(2,1)S(1)}, u32[]{:S(2)}, u32[]{:S(2)}) %collective-permute-start) | collective-permute-done | bytes 294944 | tf_op jit(solution)/shard_map/ppermute | solution.py:373
  58.1 3.2 %collective-permute-start.9 = (bf16[144,16,128]{2,1,0:T(8,128)(2,1)S(1)}, bf16[144,16,128]{2,1,0:T(8,128)(2,1)S(1)}, u32[]{:S(2)}, u32[]{:S(2)}) collective-permute-start(bf16[144,16,128]{2,1,0:T(8,128)(2,1)S(1)} %constant_dynamic-update-slice_fusion.refs_1_), channel_id=1, source_target_pairs={{0,1},{1,0},{2,3},{3,2},{4,5},{5,4},{6,7},{7,6},{8,9},{9,8},{10,11... | collective-permute-start | bytes 1769480 | tf_op jit(solution)/shard_map/ppermute | solution.py:373
  61.4 1.5 collective-permute-start.3
  62.9 3.5 %collective-permute-done.2 = bf16[72,16,128]{2,1,0:T(8,128)(2,1)S(1)} collective-permute-done((bf16[72,16,128]{2,1,0:T(8,128)(2,1)S(1)}, bf16[72,16,128]{2,1,0:T(8,128)(2,1)S(1)}, u32[]{:S(2)}, u32[]{:S(2)}) %collective-permute-start.2) | collective-permute-done | bytes 294944 | tf_op jit(solution)/shard_map/ppermute | solution.py:373
  66.5 9.7 %collective-permute-start.10 = (bf16[144,16,128]{2,1,0:T(8,128)(2,1)S(1)}, bf16[144,16,128]{2,1,0:T(8,128)(2,1)S(1)}, u32[]{:S(2)}, u32[]{:S(2)}) collective-permute-start(bf16[144,16,128]{2,1,0:T(8,128)(2,1)S(1)} %constant_dynamic-update-slice_fusion.2.refs_2_), channel_id=1, source_target_pairs={{0,1},{1,0},{2,3},{3,2},{4,5},{5,4},{6,7},{7,6},{8,9},{9,8},{10,11... | collective-permute-start | bytes 1769480 | tf_op jit(solution)/shard_map/ppermute | solution.py:373
  76.3 8.9 %collective-permute-done.5.refs_5_ = bf16[144,16,128]{2,1,0:T(8,128)(2,1)S(1)} collective-permute-done((bf16[144,16,128]{2,1,0:T(8,128)(2,1)S(1)}, bf16[144,16,128]{2,1,0:T(8,128)(2,1)S(1)}, u32[]{:S(2)}, u32[]{:S(2)}) %collective-permute-start.5) | collective-permute-done | bytes 589856 | tf_op jit(solution)/shard_map/ppermute | solution.py:373
  85.3 6.2 %collective-permute-done.6.refs_6_ = bf16[144,16,128]{2,1,0:T(8,128)(2,1)S(1)} collective-permute-done((bf16[144,16,128]{2,1,0:T(8,128)(2,1)S(1)}, bf16[144,16,128]{2,1,0:T(8,128)(2,1)S(1)}, u32[]{:S(2)}, u32[]{:S(2)}) %collective-permute-start.6) | collective-permute-done | bytes 589856 | tf_op jit(solution)/shard_map/ppermute | solution.py:373
  91.5 1.2 collective-permute-start.8
  93.3 3.9 %collective-permute-done.7.refs_7_ = bf16[144,16,128]{2,1,0:T(8,128)(2,1)S(1)} collective-permute-done((bf16[144,16,128]{2,1,0:T(8,128)(2,1)S(1)}, bf16[144,16,128]{2,1,0:T(8,128)(2,1)S(1)}, u32[]{:S(2)}, u32[]{:S(2)}) %collective-permute-start.7) | collective-permute-done | bytes 589856 | tf_op jit(solution)/shard_map/ppermute | solution.py:373
  97.3 3.0 %collective-permute-done.8.refs_8_ = bf16[144,16,128]{2,1,0:T(8,128)(2,1)S(1)} collective-permute-done((bf16[144,16,128]{2,1,0:T(8,128)(2,1)S(1)}, bf16[144,16,128]{2,1,0:T(8,128)(2,1)S(1)}, u32[]{:S(2)}, u32[]{:S(2)}) %collective-permute-start.8) | collective-permute-done | bytes 589856 | tf_op jit(solution)/shard_map/ppermute | solution.py:373
  100.3 0.7 copy-done.17
  101.6 0.8 copy-done.21
  102.5 22.8 %shard_map.76 = (bf16[36864,128]{1,0:T(8,128)(2,1)}, bf16[12288,128]{1,0:T(8,128)(2,1)}, f32[1152,128]{1,0:T(8,128)}, f32[1152,128]{1,0:T(8,128)}) custom-call(s32[26]{0:T(128)} %copy-done.5, bf16[144,16,128]{2,1,0:T(8,128)(2,1)} %copy-done.8, bf16[144,16,128]{2,1,0:T(8,128)(2,1)} %copy-done.7, bf16[144,16,128]{2,1,0:T(8,128)(2,1)} %copy-done.11, ...), custom_call_target="tpu_custom_call" | custom-call | flops 9299999744 | bytes 20000000 | tf_op jit(solution)/shard_map/pallas_call | solution.py:389
  125.5 0.5 collective-permute-start.18
  126.0 20.9 %shard_map.77 = (bf16[36864,128]{1,0:T(8,128)(2,1)}, f32[1152,128]{1,0:T(8,128)}) custom-call(s32[26]{0:T(128)} %copy-done.5, bf16[144,16,128]{2,1,0:T(8,128)(2,1)} %copy-done.8, bf16[144,16,128]{2,1,0:T(8,128)(2,1)} %copy-done.7, bf16[144,16,128]{2,1,0:T(8,128)(2,1)} %copy-done.11, ...), custom_call_target="tpu_custom_call", output_to_operand_aliasing={{0}: (18, {})} | custom-call | flops 9299999744 | bytes 20000000 | tf_op jit(solution)/shard_map/pallas_call | solution.py:400
  146.9 1.1 copy-done.2
  148.0 1.1 copy-done.3
  149.0 3.8 %shard_map.78 = (bf16[36864,128]{1,0:T(8,128)(2,1)}, f32[1152,128]{1,0:T(8,128)}, f32[1152,128]{1,0:T(8,128)}) custom-call(s32[26]{0:T(128)S(1)} %copy-done.6, bf16[36864,128]{1,0:T(8,128)(2,1)} %get-tuple-element.18._, bf16[12288,128]{1,0:T(8,128)(2,1)S(1)} %collective-permute-done.17.received, ...), custom_call_target="tpu_custom_call", output_to_operand_aliasing={{0}: (1, {})} | custom-call | tf_op jit(solution)/shard_map/pallas_call | solution.py:410
  (71 shorter events, 2.1 us)
Async XLA Ops:
  7.2 95.3 %all-gather.2.cloned.1.call-start = ((), (), s32[]{:S(2)}) async-start(), calls=%async_computation.2 | async-start | bytes 9732096 | tf_op jit(solution)/shard_map/all_gather | solution.py:354
  12.1 15.5 %all-to-all-start = ((f32[32,1,128]{2,1,0:T(1,128)}), f32[32,1,128]{2,1,0:T(1,128)S(1)}, u32[]{:S(2)}, u32[]{:S(2)}) async-start(f32[32,1,128]{2,1,0:T(1,128)} %broadcast_in_dim.4), calls=%async_computation | async-start | bytes 32768 | tf_op jit(solution)/shard_map/all_to_all | solution.py:358
  28.2 14.6 %all-to-all-start.1 = ((f32[8,1,128]{2,1,0:T(1,128)}), f32[8,1,128]{2,1,0:T(1,128)S(1)}, u32[]{:S(2)}, u32[]{:S(2)}) async-start(f32[8,1,128]{2,1,0:T(1,128)} %broadcast_in_dim.10), calls=%async_computation.1 | async-start | bytes 8192 | tf_op jit(solution)/shard_map/all_to_all | solution.py:360
  37.1 65.3 %copy-start.5 = (s32[26]{0:T(128)}, s32[26]{0:T(128)S(1)}, u32[]{:S(2)}) copy-start(s32[26]{0:T(128)S(1)} %pad_add_fusion.info.refs_0_) | copy-start | bytes 316
  46.8 11.3 %collective-permute-start = (bf16[72,16,128]{2,1,0:T(8,128)(2,1)S(1)}, bf16[72,16,128]{2,1,0:T(8,128)(2,1)S(1)}, u32[]{:S(2)}, u32[]{:S(2)}) collective-permute-start(bf16[72,16,128]{2,1,0:T(8,128)(2,1)S(1)} %get-tuple-element.16), channel_id=1, source_target_pairs={{0,2},{1,9},{2,4},{3,11},{4,6},{5,13},{6,0},{7,15},{8,10},{9,17},{... | collective-permute-start | bytes 884744 | tf_op jit(solution)/shard_map/ppermute | solution.py:373
  47.2 15.7 %collective-permute-start.1 = (bf16[72,16,128]{2,1,0:T(8,128)(2,1)S(1)}, bf16[72,16,128]{2,1,0:T(8,128)(2,1)S(1)}, u32[]{:S(2)}, u32[]{:S(2)}) collective-permute-start(bf16[72,16,128]{2,1,0:T(8,128)(2,1)S(1)} %get-tuple-element.16), channel_id=1, source_target_pairs={{0,4},{1,17},{2,6},{3,19},{4,0},{5,21},{6,2},{7,23},{8,12},{9,25},... | collective-permute-start | bytes 884744 | tf_op jit(solution)/shard_map/ppermute | solution.py:373
  48.8 17.6 %collective-permute-start.2 = (bf16[72,16,128]{2,1,0:T(8,128)(2,1)S(1)}, bf16[72,16,128]{2,1,0:T(8,128)(2,1)S(1)}, u32[]{:S(2)}, u32[]{:S(2)}) collective-permute-start(bf16[72,16,128]{2,1,0:T(8,128)(2,1)S(1)} %get-tuple-element.16), channel_id=1, source_target_pairs={{0,6},{1,25},{2,0},{3,27},{4,2},{5,29},{6,4},{7,31},{8,14},{9,1},{... | collective-permute-start | bytes 884744 | tf_op jit(solution)/shard_map/ppermute | solution.py:373
  58.1 44.3 %copy-start.8 = (bf16[144,16,128]{2,1,0:T(8,128)(2,1)}, bf16[144,16,128]{2,1,0:T(8,128)(2,1)S(1)}, u32[]{:S(2)}) copy-start(bf16[144,16,128]{2,1,0:T(8,128)(2,1)S(1)} %constant_dynamic-update-slice_fusion.refs_1_) | copy-start | bytes 1769476
  58.1 18.1 %collective-permute-start.9 = (bf16[144,16,128]{2,1,0:T(8,128)(2,1)S(1)}, bf16[144,16,128]{2,1,0:T(8,128)(2,1)S(1)}, u32[]{:S(2)}, u32[]{:S(2)}) collective-permute-start(bf16[144,16,128]{2,1,0:T(8,128)(2,1)S(1)} %constant_dynamic-update-slice_fusion.refs_1_), channel_id=1, source_target_pairs={{0,1},{1,0},{2,3},{3,2},{4,5},{5,4},{6,7},{7,6},{8,9},{9,8},{10,11... | collective-permute-start | bytes 1769480 | tf_op jit(solution)/shard_map/ppermute | solution.py:373
  61.4 23.8 %collective-permute-start.5 = (bf16[144,16,128]{2,1,0:T(8,128)(2,1)S(1)}, bf16[144,16,128]{2,1,0:T(8,128)(2,1)S(1)}, u32[]{:S(2)}, u32[]{:S(2)}) collective-permute-start(bf16[144,16,128]{2,1,0:T(8,128)(2,1)S(1)} %constant_dynamic-update-slice_fusion.refs_1_), channel_id=1, source_target_pairs={{0,24},{1,7},{2,26},{3,1},{4,28},{5,3},{6,30},{7,5},{8,0},{9,15},{... | collective-permute-start | bytes 1769480 | tf_op jit(solution)/shard_map/ppermute | solution.py:373
  61.4 23.8 %collective-permute-start.3 = (bf16[144,16,128]{2,1,0:T(8,128)(2,1)S(1)}, bf16[144,16,128]{2,1,0:T(8,128)(2,1)S(1)}, u32[]{:S(2)}, u32[]{:S(2)}) collective-permute-start(bf16[144,16,128]{2,1,0:T(8,128)(2,1)S(1)} %constant_dynamic-update-slice_fusion.refs_1_), channel_id=1, source_target_pairs={{0,8},{1,3},{2,10},{3,5},{4,12},{5,7},{6,14},{7,1},{8,16},{9,11},{... | collective-permute-start | bytes 1769480 | tf_op jit(solution)/shard_map/ppermute | solution.py:373
  66.4 36.0 %copy-start.7 = (bf16[144,16,128]{2,1,0:T(8,128)(2,1)}, bf16[144,16,128]{2,1,0:T(8,128)(2,1)S(1)}, u32[]{:S(2)}) copy-start(bf16[144,16,128]{2,1,0:T(8,128)(2,1)S(1)} %constant_dynamic-update-slice_fusion.2.refs_2_) | copy-start | bytes 1769476
  66.4 25.0 %collective-permute-start.6 = (bf16[144,16,128]{2,1,0:T(8,128)(2,1)S(1)}, bf16[144,16,128]{2,1,0:T(8,128)(2,1)S(1)}, u32[]{:S(2)}, u32[]{:S(2)}) collective-permute-start(bf16[144,16,128]{2,1,0:T(8,128)(2,1)S(1)} %constant_dynamic-update-slice_fusion.2.refs_2_), channel_id=1, source_target_pairs={{0,24},{1,7},{2,26},{3,1},{4,28},{5,3},{6,30},{7,5},{8,0},{9,15},{... | collective-permute-start | bytes 1769480 | tf_op jit(solution)/shard_map/ppermute | solution.py:373
  66.5 26.2 %collective-permute-start.10 = (bf16[144,16,128]{2,1,0:T(8,128)(2,1)S(1)}, bf16[144,16,128]{2,1,0:T(8,128)(2,1)S(1)}, u32[]{:S(2)}, u32[]{:S(2)}) collective-permute-start(bf16[144,16,128]{2,1,0:T(8,128)(2,1)S(1)} %constant_dynamic-update-slice_fusion.2.refs_2_), channel_id=1, source_target_pairs={{0,1},{1,0},{2,3},{3,2},{4,5},{5,4},{6,7},{7,6},{8,9},{9,8},{10,11... | collective-permute-start | bytes 1769480 | tf_op jit(solution)/shard_map/ppermute | solution.py:373
  76.3 26.2 %copy-start.9 = (bf16[144,16,128]{2,1,0:T(8,128)(2,1)}, bf16[144,16,128]{2,1,0:T(8,128)(2,1)S(1)}, u32[]{:S(2)}) copy-start(bf16[144,16,128]{2,1,0:T(8,128)(2,1)S(1)} %collective-permute-done.9.refs_9_) | copy-start | bytes 1769476
  76.3 16.5 %collective-permute-start.4 = (bf16[144,16,128]{2,1,0:T(8,128)(2,1)S(1)}, bf16[144,16,128]{2,1,0:T(8,128)(2,1)S(1)}, u32[]{:S(2)}, u32[]{:S(2)}) collective-permute-start(bf16[144,16,128]{2,1,0:T(8,128)(2,1)S(1)} %constant_dynamic-update-slice_fusion.2.refs_2_), channel_id=1, source_target_pairs={{0,8},{1,3},{2,10},{3,5},{4,12},{5,7},{6,14},{7,1},{8,16},{9,11},{... | collective-permute-start | bytes 1769480 | tf_op jit(solution)/shard_map/ppermute | solution.py:373
  85.1 17.3 %copy-start.10 = (bf16[144,16,128]{2,1,0:T(8,128)(2,1)}, bf16[144,16,128]{2,1,0:T(8,128)(2,1)S(1)}, u32[]{:S(2)}) copy-start(bf16[144,16,128]{2,1,0:T(8,128)(2,1)S(1)} %collective-permute-done.5.refs_5_) | copy-start | bytes 1769476
  85.1 8.1 %collective-permute-start.13 = (bf16[144,16,128]{2,1,0:T(8,128)(2,1)S(1)}, bf16[144,16,128]{2,1,0:T(8,128)(2,1)S(1)}, u32[]{:S(2)}, u32[]{:S(2)}) collective-permute-start(bf16[144,16,128]{2,1,0:T(8,128)(2,1)S(1)} %collective-permute-done.5.refs_5_), channel_id=1, source_target_pairs={{0,1},{1,0},{2,3},{3,2},{4,5},{5,4},{6,7},{7,6},{8,9},{9,8},{10,11... | collective-permute-start | bytes 1769480 | tf_op jit(solution)/shard_map/ppermute | solution.py:373
  85.2 17.3 %copy-start.11 = (bf16[144,16,128]{2,1,0:T(8,128)(2,1)}, bf16[144,16,128]{2,1,0:T(8,128)(2,1)S(1)}, u32[]{:S(2)}) copy-start(bf16[144,16,128]{2,1,0:T(8,128)(2,1)S(1)} %collective-permute-done.3.refs_3_) | copy-start | bytes 1769476
  85.2 12.1 %collective-permute-start.7 = (bf16[144,16,128]{2,1,0:T(8,128)(2,1)S(1)}, bf16[144,16,128]{2,1,0:T(8,128)(2,1)S(1)}, u32[]{:S(2)}, u32[]{:S(2)}) collective-permute-start(bf16[144,16,128]{2,1,0:T(8,128)(2,1)S(1)} %collective-permute-done.3.refs_3_), channel_id=1, source_target_pairs={{0,8},{1,3},{2,10},{3,5},{4,12},{5,7},{6,14},{7,1},{8,16},{9,11},{... | collective-permute-start | bytes 1769480 | tf_op jit(solution)/shard_map/ppermute | solution.py:373
  91.5 11.0 %copy-start.12 = (bf16[144,16,128]{2,1,0:T(8,128)(2,1)}, bf16[144,16,128]{2,1,0:T(8,128)(2,1)S(1)}, u32[]{:S(2)}) copy-start(bf16[144,16,128]{2,1,0:T(8,128)(2,1)S(1)} %collective-permute-done.6.refs_6_) | copy-start | bytes 1769476
  91.5 8.7 %collective-permute-start.8 = (bf16[144,16,128]{2,1,0:T(8,128)(2,1)S(1)}, bf16[144,16,128]{2,1,0:T(8,128)(2,1)S(1)}, u32[]{:S(2)}, u32[]{:S(2)}) collective-permute-start(bf16[144,16,128]{2,1,0:T(8,128)(2,1)S(1)} %collective-permute-done.6.refs_6_), channel_id=1, source_target_pairs={{0,24},{1,7},{2,26},{3,1},{4,28},{5,3},{6,30},{7,5},{8,0},{9,15},{... | collective-permute-start | bytes 1769480 | tf_op jit(solution)/shard_map/ppermute | solution.py:373
  92.7 7.5 %collective-permute-start.11 = (bf16[144,16,128]{2,1,0:T(8,128)(2,1)S(1)}, bf16[144,16,128]{2,1,0:T(8,128)(2,1)S(1)}, u32[]{:S(2)}, u32[]{:S(2)}) collective-permute-start(bf16[144,16,128]{2,1,0:T(8,128)(2,1)S(1)} %collective-permute-done.3.refs_3_), channel_id=1, source_target_pairs={{0,1},{1,0},{2,3},{3,2},{4,5},{5,4},{6,7},{7,6},{8,9},{9,8},{10,11... | collective-permute-start | bytes 1769480 | tf_op jit(solution)/shard_map/ppermute | solution.py:373
  92.7 7.5 %copy-start.14 = (bf16[144,16,128]{2,1,0:T(8,128)(2,1)}, bf16[144,16,128]{2,1,0:T(8,128)(2,1)S(1)}, u32[]{:S(2)}) copy-start(bf16[144,16,128]{2,1,0:T(8,128)(2,1)S(1)} %collective-permute-done.4.refs_4_) | copy-start | bytes 1769476
  92.7 7.5 %collective-permute-start.14 = (bf16[144,16,128]{2,1,0:T(8,128)(2,1)S(1)}, bf16[144,16,128]{2,1,0:T(8,128)(2,1)S(1)}, u32[]{:S(2)}, u32[]{:S(2)}) collective-permute-start(bf16[144,16,128]{2,1,0:T(8,128)(2,1)S(1)} %collective-permute-done.6.refs_6_), channel_id=1, source_target_pairs={{0,1},{1,0},{2,3},{3,2},{4,5},{5,4},{6,7},{7,6},{8,9},{9,8},{10,11... | collective-permute-start | bytes 1769480 | tf_op jit(solution)/shard_map/ppermute | solution.py:373
  93.2 7.0 %collective-permute-start.12 = (bf16[144,16,128]{2,1,0:T(8,128)(2,1)S(1)}, bf16[144,16,128]{2,1,0:T(8,128)(2,1)S(1)}, u32[]{:S(2)}, u32[]{:S(2)}) collective-permute-start(bf16[144,16,128]{2,1,0:T(8,128)(2,1)S(1)} %collective-permute-done.4.refs_4_), channel_id=1, source_target_pairs={{0,1},{1,0},{2,3},{3,2},{4,5},{5,4},{6,7},{7,6},{8,9},{9,8},{10,11... | collective-permute-start | bytes 1769480 | tf_op jit(solution)/shard_map/ppermute | solution.py:373
  97.2 3.0 %collective-permute-start.15 = (bf16[144,16,128]{2,1,0:T(8,128)(2,1)S(1)}, bf16[144,16,128]{2,1,0:T(8,128)(2,1)S(1)}, u32[]{:S(2)}, u32[]{:S(2)}) collective-permute-start(bf16[144,16,128]{2,1,0:T(8,128)(2,1)S(1)} %collective-permute-done.7.refs_7_), channel_id=1, source_target_pairs={{0,1},{1,0},{2,3},{3,2},{4,5},{5,4},{6,7},{7,6},{8,9},{9,8},{10,11... | collective-permute-start | bytes 1769480 | tf_op jit(solution)/shard_map/ppermute | solution.py:373
  100.2 2.2 %collective-permute-start.16 = (bf16[144,16,128]{2,1,0:T(8,128)(2,1)S(1)}, bf16[144,16,128]{2,1,0:T(8,128)(2,1)}, u32[]{:S(2)}, u32[]{:S(2)}) collective-permute-start(bf16[144,16,128]{2,1,0:T(8,128)(2,1)S(1)} %collective-permute-done.8.refs_8_), channel_id=1, source_target_pairs={{0,1},{1,0},{2,3},{3,2},{4,5},{5,4},{6,7},{7,6},{8,9},{9,8},{10,11... | collective-permute-start | bytes 1769480 | tf_op jit(solution)/shard_map/ppermute | solution.py:373
  125.4 21.5 %collective-permute-start.17 = (bf16[12288,128]{1,0:T(8,128)(2,1)}, bf16[12288,128]{1,0:T(8,128)(2,1)S(1)}, u32[]{:S(2)}, u32[]{:S(2)}) collective-permute-start(bf16[12288,128]{1,0:T(8,128)(2,1)} %get-tuple-element.19), channel_id=1, source_target_pairs={{0,1},{1,0},{2,3},{3,2},{4,5},{5,4},{6,7},{7,6},{8,9},{9,8},{10,11... | collective-permute-start | bytes 9437192 | tf_op jit(solution)/shard_map/ppermute | solution.py:373
  125.5 21.4 %collective-permute-start.18 = (f32[1152,128]{1,0:T(8,128)}, f32[1152,128]{1,0:T(8,128)}, u32[]{:S(2)}, u32[]{:S(2)}) collective-permute-start(f32[1152,128]{1,0:T(8,128)} %get-tuple-element.21), channel_id=1, source_target_pairs={{0,1},{1,0},{2,3},{3,2},{4,5},{5,4},{6,7},{7,6},{8,9},{9,8},{10,11... | collective-permute-start | bytes 1769480 | tf_op jit(solution)/shard_map/ppermute | solution.py:373
  126.0 20.9 %copy-start = (f32[147456]{0:T(1024)S(1)}, f32[147456]{0:T(1024)}, u32[]{:S(2)}) copy-start(f32[147456]{0:T(1024)} %param.6) | copy-start | bytes 1769476
  126.0 20.9 %copy-start.6 = (s32[26]{0:T(128)S(1)}, s32[26]{0:T(128)}, u32[]{:S(2)}) copy-start(s32[26]{0:T(128)} %copy-done.5) | copy-start | bytes 316
  (12 other events, 27.2 us)
Sparse Core Ops, SparseCore 0:
  11.1 76.5 all-gather.1
